TPU v7x, 512 devices: a whole 4x4x16 slice. The times are simulated.
512 devices in a mesh: dp: 4 (over x), expert: 8 (over y, core), shard: 16 (over z).
Axes of the slice: x: 4, y: 4, z: 16, core: 2. Of those that a mesh axis runs over, the one named last changes fastest.
Arguments:
- output_gradient: bfloat16 [65536, 3072], P(('dp', 'expert', 'shard')), may hold values from -24 to 24
- saved_router_scores: float32 [65536, 8], P(('dp', 'expert', 'shard')), may hold values from -8 to 8
- expert_choice_index: int32 [65536, 2], P(('dp', 'expert', 'shard')), may hold values from 0 to 7, as said below
- router_matrix: bfloat16 [8, 3072], replicated, may hold values from -0.109375 to 0.109375
- weight_normalized_entries: bfloat16 [3072, 8192], P('shard', 'expert'), may hold values from -1 to 1
- scales: bfloat16 [48, 8192], P('shard', 'expert'), may hold values from 0.0099487305 to 0.099609375
- stored_hidden_state: bfloat16 [4, 16, 256, 8192], P('dp', 'shard', None, 'expert'), may hold values from -6 to 6
- context: bfloat16 [65536, 3072], P(('dp', 'expert', 'shard')), may hold values from -6 to 6
- adapter_down_factor: bfloat16 [64, 3072], replicated, may hold values from -0.109375 to 0.109375
- adapter_up_factor: bfloat16 [64, 3072], replicated, may hold values from -0.109375 to 0.109375
Outputs:
- hidden_grad: bfloat16 [4, 16, 256, 8192], P('dp', 'shard', None, 'expert')
- token_grad: bfloat16 [65536, 3072], P(('dp', 'expert', 'shard'))
- grad_down: float32 [64, 3072], P(None, 'shard')
- up_factor_gradient: float32 [64, 3072], P(None, 'shard')
Inputs may be any that keep to these rules, and one draw needn't show every extreme that they name: `expert_choice_index`: each token names two different experts and expert 0 at most once. The 128 tokens of one device block name expert 0 at most 32 times, and in every draw all device blocks of some pair of dp and shard indices name it exactly 32 times.
All inputs are finite; a program needn't handle non-finite values.
Results may differ from a plain program's by a relative error of at most 0.015.
Values may be sent and summed in bfloat16 or wider, within the bound.
A program may use at most 64 MiB of HBM per device.

v0:
```python
import jax
import jax.numpy as jnp
from jax import lax
from jax.sharding import PartitionSpec as P

ADAPTER_SCALE = 0.25


def per_device(
    output_gradient,
    saved_router_scores,
    expert_choice_index,
    router_matrix,
    weight_normalized_entries,
    scales,
    stored_hidden_state,
    context,
    adapter_down_factor,
    adapter_up_factor,
):
    expert_count = lax.axis_size("expert")
    shard_count = lax.axis_size("shard")
    tokens, feature_width = output_gradient.shape
    experts = saved_router_scores.shape[1]
    row_count = stored_hidden_state.shape[2]
    capacity = row_count // expert_count
    ff_share = stored_hidden_state.shape[3]
    block_size = weight_normalized_entries.shape[0] // scales.shape[0]
    labels = jnp.arange(experts, dtype=jnp.int32)
    choose = expert_choice_index[:, :, None] == labels[None, None, :]
    chosen = jnp.sum(jnp.where(choose, saved_router_scores[:, None, :], 0.0), axis=2)
    first_prob = 1.0 / (1.0 + jnp.exp(chosen[:, 1] - chosen[:, 0]))
    second_prob = 1.0 - first_prob
    in_window = expert_choice_index == 0
    window_flag = jnp.any(in_window, axis=1)
    flag_int = window_flag.astype(jnp.int32)
    slot_index = jnp.cumsum(flag_int) - flag_int
    route_probs = jnp.stack([first_prob, second_prob], axis=1).astype(jnp.bfloat16)
    window_prob = jnp.where(in_window[:, 0], route_probs[:, 0], route_probs[:, 1])
    slot_labels = jnp.arange(capacity, dtype=jnp.int32)
    placement = (window_flag[None, :] & (slot_index[None, :] == slot_labels[:, None])).astype(
        jnp.bfloat16
    )
    send_rows = jnp.dot(placement, output_gradient, preferred_element_type=jnp.float32).astype(
        jnp.bfloat16
    )
    send_probs = jnp.dot(placement, window_prob, preferred_element_type=jnp.float32).astype(
        jnp.bfloat16
    )
    all_rows, all_probs = (
        lax.all_gather(send_rows, "expert", axis=0, tiled=True),
        lax.all_gather(send_probs, "expert", axis=0, tiled=True),
    )
    code_blocks = weight_normalized_entries.reshape(scales.shape[0], block_size, ff_share)
    own_weight = (
        (code_blocks.astype(jnp.float32) * scales.astype(jnp.float32)[:, None, :])
        .astype(jnp.bfloat16)
        .reshape(weight_normalized_entries.shape[0], ff_share)
    )
    product = jnp.dot(
        all_rows,
        lax.all_gather(own_weight, "shard", axis=0, tiled=True),
        preferred_element_type=jnp.float32,
    )
    hidden_grad = (all_probs.astype(jnp.float32)[:, None] * product).astype(jnp.bfloat16)
    partial_value = jnp.sum(stored_hidden_state[0, 0].astype(jnp.float32) * product, axis=1)
    returned = lax.psum_scatter(partial_value, "expert", scatter_dimension=0, tiled=True)
    window_grad = jnp.where(window_flag, returned[jnp.minimum(slot_index, capacity - 1)], 0.0)
    pair_grad = jnp.where(in_window, window_grad[:, None], 0.0)
    spread = first_prob * second_prob * (pair_grad[:, 0] - pair_grad[:, 1])
    sign_table = choose[:, 0, :].astype(jnp.float32) - choose[:, 1, :].astype(jnp.float32)
    logit_grad = (spread[:, None] * sign_table).astype(jnp.bfloat16)
    token_grad = jnp.dot(logit_grad, router_matrix, preferred_element_type=jnp.float32).astype(
        jnp.bfloat16
    )
    token_kept = lax.optimization_barrier(token_grad)
    residual_gradient = (
        output_gradient.astype(jnp.float32) + token_kept.astype(jnp.float32)
    ).astype(jnp.bfloat16)
    narrow_input = lax.dot_general(
        context, adapter_down_factor, (((1,), (1,)), ((), ())), preferred_element_type=jnp.float32
    ).astype(jnp.bfloat16)
    narrow_gradient = (
        ADAPTER_SCALE
        * lax.dot_general(
            residual_gradient,
            adapter_up_factor,
            (((1,), (1,)), ((), ())),
            preferred_element_type=jnp.float32,
        )
    ).astype(jnp.bfloat16)
    partial_up_gradient = ADAPTER_SCALE * lax.dot_general(
        narrow_input,
        residual_gradient,
        (((0,), (0,)), ((), ())),
        preferred_element_type=jnp.float32,
    )
    part_down = lax.dot_general(
        narrow_gradient, context, (((0,), (0,)), ((), ())), preferred_element_type=jnp.float32
    )
    summed_up, summed_down = lax.psum((partial_up_gradient, part_down), ("dp", "expert", "shard"))
    share_width = feature_width // shard_count
    first_col = lax.axis_index("shard") * share_width
    up_factor_gradient = lax.dynamic_slice_in_dim(summed_up, first_col, share_width, 1)
    grad_down = lax.dynamic_slice_in_dim(summed_down, first_col, share_width, 1)
    return (
        hidden_grad.reshape(stored_hidden_state.shape),
        token_grad,
        grad_down,
        up_factor_gradient,
    )


def solution(mesh):
    in_specs = (
        P(("dp", "expert", "shard"), None),
        P(("dp", "expert", "shard"), None),
        P(("dp", "expert", "shard"), None),
        P(),
        P("shard", "expert"),
        P("shard", "expert"),
        P("dp", "shard", None, "expert"),
        P(("dp", "expert", "shard"), None),
        P(),
        P(),
    )
    out_specs = (
        P("dp", "shard", None, "expert"),
        P(("dp", "expert", "shard"), None),
        P(None, "shard"),
        P(None, "shard"),
    )
    return jax.shard_map(
        per_device, mesh=mesh, in_specs=in_specs, out_specs=out_specs, check_vma=False
    )
```

profile of v0, /device:TPU:2, one launch (start us, length us, event | category | flops | bytes accessed | tf_op | source)
XLA Modules:
  0.0 639.7 jit_solution(14666868364817851319)
XLA Ops:
  7.2 0.0 copy-start
  7.2 0.0 copy-start.7
  7.2 0.0 copy-start.5
  7.2 0.0 copy-start.3
  7.2 0.0 copy-start.6
  7.2 0.0 copy-start.8
  7.2 0.0 all-gather.3.cloned.1.call-start
  7.3 0.8 fusion.24
  8.1 0.1 copy.26
  8.2 0.2 reduce-window.4
  8.4 0.1 fusion.6
  8.5 2.0 convolution_convert_fusion.1
  10.6 0.0 all-gather.3.cloned.1.call-update
  10.6 0.0 all-gather.5.cloned.1.call-start
  10.6 0.7 convert_element_type.90
  11.3 0.0 copy-done.3
  11.3 0.8 fusion.4
  12.2 0.0 all-gather.5.cloned.1.call-update
  12.2 0.0 all-reduce.5.cloned.1.call-start
  12.3 0.0 copy-done.7
  12.3 0.6 fusion.25
  13.5 0.0 copy-done.5
  13.5 0.0 copy-done.6
  13.6 0.0 copy-start.4
  13.6 33.7 %all-gather.3.cloned.1.call-done = bf16[256,3072]{1,0:T(8,128)(2,1)} async-done(((bf16[32,3072]{1,0:T(8,128)(2,1)}), bf16[256,3072]{1,0:T(8,128)(2,1)}) %all-gather.3.cloned.1.call-update) | async-done | bytes 1572880 | tf_op jit(solution)/shard_map/all_gather | solution.py:51
  47.3 89.3 %all-gather.5.cloned.1.call-done = bf16[3072,1024]{1,0:T(8,128)(2,1)} async-done(((bf16[192,1024]{1,0:T(8,128)(2,1)}), bf16[3072,1024]{1,0:T(8,128)(2,1)}) %all-gather.5.cloned.1.call-update) | async-done | bytes 6291472 | tf_op jit(solution)/shard_map/all_gather | solution.py:62
  136.5 0.0 copy-done.8
  136.5 5.2 fusion.3
  141.7 0.0 copy-start.1
  141.7 12.6 %all-reduce.1 = f32[256]{0:T(256)S(1)} all-reduce(f32[256]{0:T(256)S(1)} %get-tuple-element.14), channel_id=2, replica_groups=mesh['dp'=4,'expert'=8,'shard'=16] {'expert'}, use_global_device_ids=true, to_apply=%region_4.5.clone | all-reduce | flops 256 | bytes 2048
  154.3 0.1 dynamic-slice.2
  154.3 1.2 gather_fusion
  155.6 0.0 copy-done.4
  155.6 0.4 convolution_convert_fusion
  156.0 0.0 copy-done
  156.1 0.0 copy-done.1
  156.1 0.0 copy-start.2
  156.1 3.0 convolution_multiply_fusion
  159.0 0.0 copy-done.2
  159.0 2.7 fusion.1
  161.7 0.0 all-reduce.5.cloned.1.call-update
  162.4 0.1 fusion.2
  162.5 0.2 dynamic-update-slice
  162.7 12.4 %all-reduce = bf16[256]{0:T(256)(128)(2,1)S(1)} all-reduce(bf16[256]{0:T(256)(128)(2,1)S(1)} %dynamic-update-slice), channel_id=1, replica_groups=mesh['dp'=4,'expert'=8,'shard'=16] {'expert'}, use_global_device_ids=true, to_apply=%add | all-reduce | flops 256 | bytes 1024
  175.1 0.9 fusion.5
  176.1 455.4 %all-reduce.5.cloned.1.call-done = (f32[64,3072]{1,0:T(8,128)}, f32[64,3072]{1,0:T(8,128)}) async-done(((f32[64,3072]{1,0:T(8,128)}, f32[64,3072]{1,0:T(8,128)}), (f32[64,3072]{1,0:T(8,128)}, f32[64,3072]{1,0:T(8,128)})) %all-reduce.5.cloned.1.call-update) | async-done | bytes 1572880 | tf_op jit(solution)/shard_map/psum | solution.py:101
  631.5 1.7 constant_dynamic-slice_fusion
  (10 shorter events, 0.1 us)
Async XLA Ops:
  7.2 148.9 %copy-start = (bf16[128,3072]{1,0:T(8,128)(2,1)S(1)}, bf16[128,3072]{1,0:T(8,128)(2,1)}, u32[]{:S(2)}) copy-start(bf16[128,3072]{1,0:T(8,128)(2,1)} %param.17) | copy-start | bytes 2359300
  7.2 5.1 copy-start.7
  7.2 6.3 copy-start.5
  7.2 4.1 copy-start.3
  7.2 6.3 copy-start.6
  7.2 129.3 %copy-start.8 = (bf16[1,1,256,1024]{3,2,1,0:T(8,128)(2,1)S(1)}, bf16[1,1,256,1024]{3,2,1,0:T(8,128)(2,1)}, u32[]{:S(2)}) copy-start(bf16[1,1,256,1024]{3,2,1,0:T(8,128)(2,1)} %param.16) | copy-start | bytes 1572868
  7.2 40.0 %all-gather.3.cloned.1.call-start = ((), (), s32[]{:S(2)}) async-start(), calls=%async_computation | async-start | bytes 1769472 | tf_op jit(solution)/shard_map/all_gather | solution.py:51
  10.6 125.9 %all-gather.5.cloned.1.call-start = ((), (), s32[]{:S(2)}) async-start(), calls=%async_computation.1 | async-start | bytes 6684672 | tf_op jit(solution)/shard_map/all_gather | solution.py:62
  12.2 619.3 %all-reduce.5.cloned.1.call-start = ((), (), s32[]{:S(2)}) async-start(), calls=%async_computation.2 | async-start | bytes 3145728 | tf_op jit(solution)/shard_map/psum | solution.py:101
  13.6 142.0 %copy-start.4 = (bf16[8,3072]{1,0:T(8,128)(2,1)S(1)}, bf16[8,3072]{1,0:T(8,128)(2,1)}, u32[]{:S(2)}) copy-start(bf16[8,3072]{1,0:T(8,128)(2,1)} %param.13) | copy-start | bytes 147460
  141.7 14.4 %copy-start.1 = (bf16[128,3072]{1,0:T(8,128)(2,1)S(1)}, bf16[128,3072]{1,0:T(8,128)(2,1)}, u32[]{:S(2)}) copy-start(bf16[128,3072]{1,0:T(8,128)(2,1)} %param.10) | copy-start | bytes 2359300
  156.1 3.0 copy-start.2
Sparse Core Ops, SparseCore 0:
  10.8 36.4 all-gather.2
  49.9 86.5 all-gather.4
  161.9 469.5 all-reduce.4
where the time goes:
time: 640 us
  waiting for transfers between devices  578 us (90%)
  blocking collectives  25 us (4%)
  between operations  15.2 us (2%)
  matrix products  13.4 us (2%)
    psum x1, waiting for transfers between devices, per_device(): lax.psum((partial_up_gradient, part_down), ('dp', 'expert', 'shard'))  455 us
    all_gather x1, waiting for transfers between devices, per_device(): lax.all_gather(own_weight, 'shard', axis=0, tiled=True)  89.3 us
    all_gather x1, waiting for transfers between devices, per_device(): lax.all_gather(send_rows, 'expert', axis=0, tiled=True)  33.7 us
    unnamed x2, blocking collectives  25 us
  transfers between devices with their start and end apart: 3, of which 3 were waited for; matrix products, arithmetic and copies ran while one was open for 1% of the time, Pallas kernels for 0%

commit v1 on v0

--- a/solution.py
+++ b/solution.py
@@ -98,7 +98,9 @@
     part_down = lax.dot_general(
         narrow_gradient, context, (((0,), (0,)), ((), ())), preferred_element_type=jnp.float32
     )
-    summed_up, summed_down = lax.psum((partial_up_gradient, part_down), ("dp", "expert", "shard"))
+    summed_up, summed_down = lax.psum(
+        lax.psum((partial_up_gradient, part_down), ("expert", "shard")), "dp"
+    )
     share_width = feature_width // shard_count
     first_col = lax.axis_index("shard") * share_width
     up_factor_gradient = lax.dynamic_slice_in_dim(summed_up, first_col, share_width, 1)

time: 640 us -> 579 us (0.905)
  the two profiles are of different devices: /device:TPU:2 before, /device:TPU:1 now
where the time goes in v1:
time: 579 us
  waiting for transfers between devices  513 us (89%)
  blocking collectives  29.2 us (5%)
  between operations  15.3 us (3%)
  matrix products  13.4 us (2%)
    psum x1, waiting for transfers between devices, per_device(): lax.psum((partial_up_gradient, part_down), ('expert', 'shard'))  340 us
    all_gather x1, waiting for transfers between devices, per_device(): lax.all_gather(own_weight, 'shard', axis=0, tiled=True)  86.7 us
    psum x1, waiting for transfers between devices, per_device(): lax.psum(lax.psum((partial_up_gradient, part_down), ('expert', 'shard')),...  52.1 us
    all_gather x1, waiting for transfers between devices, per_device(): lax.all_gather(send_rows, 'expert', axis=0, tiled=True)  35 us
    unnamed x2, blocking collectives  29.2 us
  transfers between devices with their start and end apart: 4, of which 4 were waited for; matrix products, arithmetic and copies ran while one was open for 1% of the time, Pallas kernels for 0%

profile of v1, /device:TPU:1, one launch (start us, length us, event | category | flops | bytes accessed | tf_op | source)
XLA Modules:
  0.0 578.9 jit_solution(14014285429382318275)
XLA Ops:
  7.2 0.0 copy-start
  7.2 0.0 copy-start.7
  7.2 0.0 copy-start.5
  7.2 0.0 copy-start.3
  7.2 0.0 copy-start.6
  7.2 0.0 copy-start.8
  7.2 0.0 all-gather.3.cloned.1.call-start
  7.3 0.8 fusion.24
  8.1 0.1 copy.26
  8.2 0.2 reduce-window.4
  8.4 0.1 fusion.6
  8.5 2.0 convolution_convert_fusion.1
  10.6 0.0 all-gather.3.cloned.1.call-update
  10.6 0.0 all-gather.5.cloned.1.call-start
  10.6 0.7 convert_element_type.90
  11.3 0.0 copy-done.3
  11.3 0.8 fusion.4
  12.2 0.0 all-gather.5.cloned.1.call-update
  12.2 0.0 all-reduce.7.cloned.1.call-start
  12.3 0.0 copy-done.7
  12.3 0.6 fusion.25
  13.5 0.0 copy-done.5
  13.5 0.0 copy-done.6
  13.6 0.0 copy-start.4
  13.6 35.0 %all-gather.3.cloned.1.call-done = bf16[256,3072]{1,0:T(8,128)(2,1)} async-done(((bf16[32,3072]{1,0:T(8,128)(2,1)}), bf16[256,3072]{1,0:T(8,128)(2,1)}) %all-gather.3.cloned.1.call-update) | async-done | bytes 1572880 | tf_op jit(solution)/shard_map/all_gather | solution.py:51
  48.5 86.7 %all-gather.5.cloned.1.call-done = bf16[3072,1024]{1,0:T(8,128)(2,1)} async-done(((bf16[192,1024]{1,0:T(8,128)(2,1)}), bf16[3072,1024]{1,0:T(8,128)(2,1)}) %all-gather.5.cloned.1.call-update) | async-done | bytes 6291472 | tf_op jit(solution)/shard_map/all_gather | solution.py:62
  135.2 0.0 copy-done.8
  135.2 5.2 fusion.3
  140.4 0.0 copy-start.1
  140.4 14.6 %all-reduce.1 = f32[256]{0:T(256)S(1)} all-reduce(f32[256]{0:T(256)S(1)} %get-tuple-element.16), channel_id=2, replica_groups=mesh['dp'=4,'expert'=8,'shard'=16] {'expert'}, use_global_device_ids=true, to_apply=%region_4.5.clone | all-reduce | flops 256 | bytes 2048
  155.0 0.1 dynamic-slice.2
  155.1 1.2 gather_fusion
  156.3 0.0 copy-done.4
  156.3 0.4 convolution_convert_fusion
  156.8 0.0 copy-done
  156.8 0.0 copy-done.1
  156.8 0.0 copy-start.2
  156.8 3.0 convolution_multiply_fusion
  159.8 0.0 copy-done.2
  159.8 2.7 fusion.1
  162.4 0.0 all-reduce.7.cloned.1.call-update
  162.5 0.0 all-reduce.9.cloned.1.call-start
  162.5 339.5 %all-reduce.7.cloned.1.call-done = (f32[64,3072]{1,0:T(8,128)}, f32[64,3072]{1,0:T(8,128)}) async-done(((f32[64,3072]{1,0:T(8,128)}, f32[64,3072]{1,0:T(8,128)}), (f32[64,3072]{1,0:T(8,128)}, f32[64,3072]{1,0:T(8,128)})) %all-reduce.7.cloned.1.call-update) | async-done | bytes 1572880 | tf_op jit(solution)/shard_map/psum | solution.py:102
  502.1 0.0 all-reduce.9.cloned.1.call-update
  502.7 0.1 fusion.2
  502.9 0.2 dynamic-update-slice
  503.0 14.6 %all-reduce = bf16[256]{0:T(256)(128)(2,1)S(1)} all-reduce(bf16[256]{0:T(256)(128)(2,1)S(1)} %dynamic-update-slice), channel_id=1, replica_groups=mesh['dp'=4,'expert'=8,'shard'=16] {'expert'}, use_global_device_ids=true, to_apply=%add | all-reduce | flops 256 | bytes 1024
  517.7 0.9 fusion.5
  518.6 52.1 %all-reduce.9.cloned.1.call-done = (f32[64,3072]{1,0:T(8,128)}, f32[64,3072]{1,0:T(8,128)}) async-done(((f32[64,3072]{1,0:T(8,128)}, f32[64,3072]{1,0:T(8,128)}), (f32[64,3072]{1,0:T(8,128)}, f32[64,3072]{1,0:T(8,128)})) %all-reduce.9.cloned.1.call-update) | async-done | bytes 1572880 | tf_op jit(solution)/shard_map/psum | solution.py:101
  570.7 1.7 constant_dynamic-slice_fusion
  (10 shorter events, 0.1 us)
Async XLA Ops:
  7.2 149.6 %copy-start = (bf16[128,3072]{1,0:T(8,128)(2,1)S(1)}, bf16[128,3072]{1,0:T(8,128)(2,1)}, u32[]{:S(2)}) copy-start(bf16[128,3072]{1,0:T(8,128)(2,1)} %param.17) | copy-start | bytes 2359300
  7.2 5.1 copy-start.7
  7.2 6.3 %copy-start.5 = (s32[128,2]{0,1:T(2,128)S(1)}, s32[128,2]{0,1:T(2,128)}, u32[]{:S(2)}) copy-start(s32[128,2]{0,1:T(2,128)} %param.12) | copy-start | bytes 3076
  7.2 4.1 copy-start.3
  7.2 6.3 %copy-start.6 = (f32[128,8]{0,1:T(8,128)S(1)}, f32[128,8]{0,1:T(8,128)}, u32[]{:S(2)}) copy-start(f32[128,8]{0,1:T(8,128)} %param.11) | copy-start | bytes 12292
  7.2 128.0 %copy-start.8 = (bf16[1,1,256,1024]{3,2,1,0:T(8,128)(2,1)S(1)}, bf16[1,1,256,1024]{3,2,1,0:T(8,128)(2,1)}, u32[]{:S(2)}) copy-start(bf16[1,1,256,1024]{3,2,1,0:T(8,128)(2,1)} %param.16) | copy-start | bytes 1572868
  7.2 41.3 %all-gather.3.cloned.1.call-start = ((), (), s32[]{:S(2)}) async-start(), calls=%async_computation | async-start | bytes 1769472 | tf_op jit(solution)/shard_map/all_gather | solution.py:51
  10.6 124.6 %all-gather.5.cloned.1.call-start = ((), (), s32[]{:S(2)}) async-start(), calls=%async_computation.1 | async-start | bytes 6684672 | tf_op jit(solution)/shard_map/all_gather | solution.py:62
  12.2 489.9 %all-reduce.7.cloned.1.call-start = ((), (), s32[]{:S(2)}) async-start(), calls=%async_computation.2 | async-start | bytes 3145728 | tf_op jit(solution)/shard_map/psum | solution.py:102
  13.6 142.8 %copy-start.4 = (bf16[8,3072]{1,0:T(8,128)(2,1)S(1)}, bf16[8,3072]{1,0:T(8,128)(2,1)}, u32[]{:S(2)}) copy-start(bf16[8,3072]{1,0:T(8,128)(2,1)} %param.13) | copy-start | bytes 147460
  140.4 16.4 %copy-start.1 = (bf16[128,3072]{1,0:T(8,128)(2,1)S(1)}, bf16[128,3072]{1,0:T(8,128)(2,1)}, u32[]{:S(2)}) copy-start(bf16[128,3072]{1,0:T(8,128)(2,1)} %param.10) | copy-start | bytes 2359300
  156.8 3.0 copy-start.2
  162.5 408.2 %all-reduce.9.cloned.1.call-start = ((), (), s32[]{:S(2)}) async-start(), calls=%async_computation.3 | async-start | bytes 3145728 | tf_op jit(solution)/shard_map/psum | solution.py:101
Sparse Core Ops, SparseCore 0:
  10.8 37.7 all-gather.2
  51.2 83.9 all-gather.4
  162.6 339.4 all-reduce.6
  504.4 66.2 all-reduce.8
